TPU v7x, 256 devices: a whole 4x4x8 slice. The times are simulated.
256 devices in a mesh: section: 4 (over x), row: 4 (over y), col: 16 (over z, core).
Axes of the slice: x: 4, y: 4, z: 8, core: 2. Of those that a mesh axis runs over, the one named last changes fastest.
Arguments:
- layer_input: bfloat16 [4, 512, 4096], P('section', 'col', 'row'), may hold values from -6 to 6
- output_grad: bfloat16 [4, 512, 4096], P('section', 'col', 'row'), may hold values from -6 to 6
- gate_weight: bfloat16 [4, 4096, 14336], P('section', 'row', 'col'), may hold values from -0.09375 to 0.09375
- up_weight: bfloat16 [4, 4096, 14336], P('section', 'row', 'col'), may hold values from -0.09375 to 0.09375
- down_weight: bfloat16 [4, 14336, 4096], P('section', 'col', 'row'), may hold values from -0.046875 to 0.046875
Outputs:
- grad_down: bfloat16 [4, 14336, 4096], P('section', 'col', 'row')
- grad_gate: bfloat16 [4, 4096, 14336], P('section', 'row', 'col')
- grad_up: bfloat16 [4, 4096, 14336], P('section', 'row', 'col')
- grad_received: bfloat16 [4, 512, 4096], P('section', 'col', 'row')
All inputs are finite; a program needn't handle non-finite values.
Results may differ from a plain program's by a relative error of at most 0.005.
Values may be sent and summed in bfloat16 or wider, within the bound.
A program may use at most 64 MiB of HBM per device.

v0:
```python
import jax
import jax.numpy as jnp
from jax import lax
from jax.sharding import PartitionSpec as P


def passed_along(block, axis, distance):
    devices = range(lax.axis_size(axis))
    route = [((i - distance) % len(devices), i) for i in devices]
    return lax.ppermute(block, axis, route)


def contract_rows(left, right):
    return lax.dot_general(
        left, right, (((0,), (0,)), ((), ())), preferred_element_type=jnp.float32
    )


def contract_cols(left, right):
    return lax.dot_general(
        left, right, (((1,), (1,)), ((), ())), preferred_element_type=jnp.float32
    )


def elementwise(summed, width):
    gate = summed[:, :width]
    up = summed[:, width : 2 * width]
    grad_hidden = summed[:, 2 * width :]
    sig = jax.nn.sigmoid(gate)
    hidden = (gate * sig * up).astype(jnp.bfloat16)
    grad_gate_in = (grad_hidden * up * sig * (1.0 + gate * (1.0 - sig))).astype(jnp.bfloat16)
    grad_up_in = (grad_hidden * gate * sig).astype(jnp.bfloat16)
    return (hidden, grad_gate_in, grad_up_in)


def shards(layer_input, output_grad, gate_weight, up_weight, down_weight):
    inputs = layer_input[0]
    grads = output_grad[0]
    w_gate = gate_weight[0]
    w_up = up_weight[0]
    w_down = down_weight[0]
    width = w_gate.shape[1]
    inputs_all, grads_all = (
        lax.all_gather(inputs, "col", axis=0, tiled=True),
        lax.all_gather(grads, "col", axis=0, tiled=True),
    )
    in_rows = inputs_all
    grad_rows = grads_all
    summed = lax.psum_scatter(
        jnp.concatenate(
            [
                jnp.dot(in_rows, w_gate, preferred_element_type=jnp.float32),
                jnp.dot(in_rows, w_up, preferred_element_type=jnp.float32),
                contract_cols(grad_rows, w_down),
            ],
            axis=1,
        ),
        "row",
        scatter_dimension=0,
        tiled=True,
    )
    pieces = elementwise(summed, width)
    hidden = lax.all_gather(pieces[0], "row", axis=0, tiled=True)
    grad_gate_in = lax.all_gather(pieces[1], "row", axis=0, tiled=True)
    grad_up_in = lax.all_gather(pieces[2], "row", axis=0, tiled=True)
    in_rows = inputs_all
    grad_rows = grads_all
    acc_down = contract_rows(hidden, grad_rows)
    acc_gate = contract_rows(in_rows, grad_gate_in)
    acc_up = contract_rows(in_rows, grad_up_in)
    rows_input = contract_cols(grad_gate_in, w_gate) + contract_cols(grad_up_in, w_up)
    acc_input = rows_input
    acc_down, acc_gate, acc_up, acc_input = (acc_down, acc_gate, acc_up, acc_input)
    input_grad = lax.psum_scatter(acc_input, "col", scatter_dimension=0, tiled=True).astype(
        jnp.bfloat16
    )
    received = passed_along(input_grad, "section", -1)
    return (
        acc_down.astype(jnp.bfloat16)[None],
        acc_gate.astype(jnp.bfloat16)[None],
        acc_up.astype(jnp.bfloat16)[None],
        received[None],
    )


def solution(mesh):
    return jax.shard_map(
        shards,
        mesh=mesh,
        in_specs=(
            P("section", "col", "row"),
            P("section", "col", "row"),
            P("section", "row", "col"),
            P("section", "row", "col"),
            P("section", "col", "row"),
        ),
        out_specs=(
            P("section", "col", "row"),
            P("section", "row", "col"),
            P("section", "row", "col"),
            P("section", "col", "row"),
        ),
        check_vma=False,
    )
```

profile of v0, /device:TPU:1, one launch (start us, length us, event | category | flops | bytes accessed | tf_op | source)
XLA Modules:
  0.0 269.4 jit_solution(15507695068676996432)
XLA Ops:
  7.2 0.0 copy-start
  7.2 0.0 all-gather.5.cloned.1.call-start
  7.2 0.7 all-gather.5.cloned.1.call-update
  7.9 0.0 all-gather.7.cloned.1.call-start
  8.0 0.7 all-gather.7.cloned.1.call-update
  8.7 0.0 reduce-scatter.3.cloned.1.call-start
  8.7 44.0 %all-gather.5.cloned.1.call-done = bf16[1,512,1024]{2,1,0:T(8,128)(2,1)} async-done(((bf16[1,32,1024]{2,1,0:T(8,128)(2,1)}), bf16[1,512,1024]{2,1,0:T(8,128)(2,1)}) %all-gather.5.cloned.1.call-update) | async-done | bytes 1048592 | tf_op jit(solution)/shard_map/all_gather | solution.py:44
  52.7 0.0 copy-done
  52.7 0.0 copy-start.4
  52.7 0.0 copy-start.6
  52.7 3.9 %fusion.4 = f32[512,896]{1,0:T(8,128)} fusion(bf16[1,1024,896]{2,1,0:T(8,128)(2,1)S(1)} %copy-done, bf16[1,512,1024]{2,1,0:T(8,128)(2,1)} %all-gather.5.cloned.1.call-done), kind=kOutput, calls=%fused_computation.5 | convolution fusion | flops 939524096 | bytes 4718592 | tf_op jit(solution)/shard_map/dot_general | solution.py:53
  56.5 0.0 copy-done.4
  56.5 0.0 copy-done.6
  56.5 2.5 fusion.8
  59.0 32.8 %all-gather.7.cloned.1.call-done = bf16[1,512,1024]{2,1,0:T(8,128)(2,1)} async-done(((bf16[1,32,1024]{2,1,0:T(8,128)(2,1)}), bf16[1,512,1024]{2,1,0:T(8,128)(2,1)}) %all-gather.7.cloned.1.call-update) | async-done | bytes 1048592 | tf_op jit(solution)/shard_map/all_gather | solution.py:45
  91.8 0.0 copy-start.1
  91.8 0.0 copy-start.2
  91.8 3.2 %fusion = f32[512,896]{1,0:T(8,128)S(1)} fusion(bf16[1,896,1024]{2,1,0:T(8,128)(2,1)} %param.9, bf16[1,512,1024]{2,1,0:T(8,128)(2,1)} %all-gather.7.cloned.1.call-done), kind=kOutput, calls=%fused_computation.1 | convolution fusion | flops 939524096 | bytes 4718592 | tf_op jit(solution)/shard_map/dot_general | solution.py:20
  95.0 0.0 copy-done.1
  95.0 0.0 copy-done.2
  95.1 2.8 %pad_maximum_fusion = f32[512,2688]{1,0:T(8,128)} fusion(f32[512,896]{1,0:T(8,128)S(1)} %fusion, f32[512,896]{1,0:T(8,128)S(1)} %copy-done.1, f32[512,896]{1,0:T(8,128)S(1)} %copy-done.2), kind=kLoop, calls=%fused_computation | loop fusion | flops 2752512 | bytes 11010048 | tf_op jit(solution)/shard_map/concatenate | solution.py:50
  97.8 0.0 reduce-scatter.3.cloned.1.call-update
  97.8 0.0 reduce-scatter.5.cloned.1.call-start
  97.9 58.5 %reduce-scatter.3.cloned.1.call-done = f32[128,2688]{1,0:T(8,128)} async-done(((f32[512,2688]{1,0:T(8,128)}), f32[128,2688]{1,0:T(8,128)}) %reduce-scatter.3.cloned.1.call-update) | async-done | bytes 1376272 | tf_op jit(solution)/shard_map/reduce_scatter | solution.py:49
  156.4 1.6 multiply_convert_fusion
  158.0 11.1 %all_gather.19 = bf16[512,896]{1,0:T(8,128)(2,1)S(1)} all-gather(bf16[128,896]{1,0:T(8,128)(2,1)S(1)} %get-tuple-element.8), channel_id=1, replica_groups=mesh['section'=4,'row'=4,'col'=16] {'row'}, dimensions={0}, use_global_device_ids=true | all-gather | bytes 1146880 | tf_op jit(solution)/shard_map/all_gather | solution.py:65
  169.1 11.7 %all_gather.18 = bf16[512,896]{1,0:T(8,128)(2,1)S(1)} all-gather(bf16[128,896]{1,0:T(8,128)(2,1)S(1)} %get-tuple-element.9), channel_id=1, replica_groups=mesh['section'=4,'row'=4,'col'=16] {'row'}, dimensions={0}, use_global_device_ids=true | all-gather | bytes 1146880 | tf_op jit(solution)/shard_map/all_gather | solution.py:64
  180.9 0.0 copy-start.3
  180.9 0.0 copy-start.5
  180.9 1.3 fusion.2
  182.1 0.0 copy-done.3
  182.1 0.5 copy-done.5
  182.7 2.6 fusion.10
  185.3 0.0 reduce-scatter.5.cloned.1.call-update
  185.3 0.0 copy-start.7
  185.3 4.0 %convert_bitcast_fusion.1 = bf16[1,1024,896]{1,2,0:T(8,128)(2,1)} fusion(bf16[512,896]{1,0:T(8,128)(2,1)} %copy-done.3, bf16[1,512,1024]{2,1,0:T(8,128)(2,1)} %all-gather.5.cloned.1.call-done), kind=kOutput, calls=%fused_computation.12 | convolution fusion | flops 940441600 | bytes 3801088 | tf_op jit(solution)/shard_map/dot_general | solution.py:14
  189.3 0.0 copy-done.7
  189.3 2.4 convert_bitcast_fusion
  191.7 10.7 %all_gather.17 = bf16[512,896]{1,0:T(8,128)(2,1)S(1)} all-gather(bf16[128,896]{1,0:T(8,128)(2,1)S(1)} %get-tuple-element.10), channel_id=1, replica_groups=mesh['section'=4,'row'=4,'col'=16] {'row'}, dimensions={0}, use_global_device_ids=true | all-gather | bytes 1146880 | tf_op jit(solution)/shard_map/all_gather | solution.py:63
  202.4 45.5 %reduce-scatter.5.cloned.1.call-done = f32[32,1024]{1,0:T(8,128)} async-done(((f32[512,1024]{1,0:T(8,128)}), f32[32,1024]{1,0:T(8,128)}) %reduce-scatter.5.cloned.1.call-update) | async-done | bytes 131088 | tf_op jit(solution)/shard_map/reduce_scatter | solution.py:74
  247.8 0.9 convert_element_type.35
  248.7 2.3 collective-permute-start
  251.1 3.6 %convert_bitcast_fusion.2 = bf16[1,896,1024]{2,1,0:T(8,128)(2,1)} fusion(bf16[512,896]{1,0:T(8,128)(2,1)S(1)} %all_gather.17, bf16[1,512,1024]{2,1,0:T(8,128)(2,1)} %all-gather.7.cloned.1.call-done), kind=kOutput, calls=%fused_computation.13 | convolution fusion | flops 940441600 | bytes 3801088 | tf_op jit(solution)/shard_map/dot_general | solution.py:14
  254.7 3.8 %copy.9 = bf16[1,1024,896]{2,1,0:T(8,128)(2,1)} copy(bf16[1,1024,896]{1,2,0:T(8,128)(2,1)} %convert_bitcast_fusion.1) | data formatting | bytes 3670016
  258.5 3.8 %copy.10 = bf16[1,1024,896]{2,1,0:T(8,128)(2,1)} copy(bf16[1,1024,896]{1,2,0:T(8,128)(2,1)} %convert_bitcast_fusion) | data formatting | bytes 3670016
  262.3 0.0 collective-permute-done
  262.3 0.6 copy.12
Async XLA Ops:
  7.2 45.5 %copy-start = (bf16[1,1024,896]{2,1,0:T(8,128)(2,1)S(1)}, bf16[1,1024,896]{2,1,0:T(8,128)(2,1)}, u32[]{:S(2)}) copy-start(bf16[1,1024,896]{2,1,0:T(8,128)(2,1)} %param.8) | copy-start | bytes 5505028
  7.2 45.5 %all-gather.5.cloned.1.call-start = ((), (), s32[]{:S(2)}) async-start(), calls=%async_computation.4 | async-start | bytes 1114112 | tf_op jit(solution)/shard_map/all_gather | solution.py:44
  7.9 83.9 %all-gather.7.cloned.1.call-start = ((), (), s32[]{:S(2)}) async-start(), calls=%async_computation.5 | async-start | bytes 1114112 | tf_op jit(solution)/shard_map/all_gather | solution.py:45
  8.7 147.8 %reduce-scatter.3.cloned.1.call-start = ((), (), s32[]{:S(2)}) async-start(), calls=%async_computation.2 | async-start | bytes 6881280 | tf_op jit(solution)/shard_map/reduce_scatter | solution.py:49
  52.7 3.9 %copy-start.4 = (bf16[1,1024,896]{2,1,0:T(8,128)(2,1)S(1)}, bf16[1,1024,896]{2,1,0:T(8,128)(2,1)}, u32[]{:S(2)}) copy-start(bf16[1,1024,896]{2,1,0:T(8,128)(2,1)} %param.7) | copy-start | bytes 5505028
  52.7 3.9 %copy-start.6 = (bf16[1,512,1024]{2,1,0:T(8,128)(2,1)S(1)}, bf16[1,512,1024]{2,1,0:T(8,128)(2,1)}, u32[]{:S(2)}) copy-start(bf16[1,512,1024]{2,1,0:T(8,128)(2,1)} %all-gather.5.cloned.1.call-done) | copy-start | bytes 3145732
  91.8 3.3 %copy-start.1 = (f32[512,896]{1,0:T(8,128)S(1)}, f32[512,896]{1,0:T(8,128)}, u32[]{:S(2)}) copy-start(f32[512,896]{1,0:T(8,128)} %fusion.4) | copy-start | bytes 5505028
  91.8 3.3 %copy-start.2 = (f32[512,896]{1,0:T(8,128)S(1)}, f32[512,896]{1,0:T(8,128)}, u32[]{:S(2)}) copy-start(f32[512,896]{1,0:T(8,128)} %fusion.8) | copy-start | bytes 5505028
  97.8 150.0 %reduce-scatter.5.cloned.1.call-start = ((), (), s32[]{:S(2)}) async-start(), calls=%async_computation.3 | async-start | bytes 2228224 | tf_op jit(solution)/shard_map/reduce_scatter | solution.py:74
  180.9 1.3 copy-start.3
  180.9 1.8 copy-start.5
  185.3 4.0 %copy-start.7 = (bf16[1,512,1024]{2,1,0:T(8,128)(2,1)S(1)}, bf16[1,512,1024]{2,1,0:T(8,128)(2,1)}, u32[]{:S(2)}) copy-start(bf16[1,512,1024]{2,1,0:T(8,128)(2,1)} %all-gather.5.cloned.1.call-done) | copy-start | bytes 3145732
  248.7 13.5 %collective-permute-start = (bf16[32,1024]{1,0:T(8,128)(2,1)S(1)}, bf16[32,1024]{1,0:T(8,128)(2,1)S(1)}, u32[]{:S(2)}, u32[]{:S(2)}) collective-permute-start(bf16[32,1024]{1,0:T(8,128)(2,1)S(1)} %convert_element_type.35), channel_id=1, source_target_pairs={{64,0},{128,64},{192,128},{0,192},{65,1},{129,65},{193,129},{1,193... | collective-permute-start | bytes 196616 | tf_op jit(solution)/shard_map/ppermute | solution.py:10
Sparse Core Ops, SparseCore 0:
  9.8 42.7 all-gather.4
  54.5 37.2 all-gather.6
  98.0 58.4 reduce-scatter.2
  185.4 62.3 reduce-scatter.4
where the time goes:
time: 272 us; the launch traced here: 269 us
  waiting for transfers between devices  182 us (67%)
  blocking collectives  33.5 us (12%)
  matrix products  23.4 us (9%)
  between operations  13.8 us (5%)
  local copies, waits for them, and re-layouts  8.8 us (3%)
  other arithmetic  5.24 us (2%)
    reduce_scatter x1, waiting for transfers between devices, shards(): lax.psum_scatter(jnp.concatenate([jnp.dot(in_rows, w_gate, preferred_elem...  58.5 us
    reduce_scatter x1, waiting for transfers between devices, shards(): lax.psum_scatter(acc_input, 'col', scatter_dimension=0, tiled=True)  45.5 us
    all_gather x1, waiting for transfers between devices, shards(): lax.all_gather(inputs, 'col', axis=0, tiled=True)  44 us
    all_gather x1, waiting for transfers between devices, shards(): lax.all_gather(grads, 'col', axis=0, tiled=True)  32.8 us
    all_gather x1, blocking collectives, shards(): grad_gate_in = lax.all_gather(pieces[1], 'row', axis=0, tiled=True)  11.7 us
    all_gather x1, blocking collectives, shards(): grad_up_in = lax.all_gather(pieces[2], 'row', axis=0, tiled=True)  11.1 us
    all_gather x1, blocking collectives, shards(): hidden = lax.all_gather(pieces[0], 'row', axis=0, tiled=True)  10.7 us
    dot_general x3, matrix products, contract_rows(): lax.dot_general(left, right, (((0,), (0,)), ((), ())), preferred_element_...  9.94 us
  transfers between devices with their start and end apart: 5, of which 4 were waited for; matrix products, arithmetic and copies ran while one was open for 9% of the time, Pallas kernels for 0%

commit v1 on v0

v1 whole, which is shorter than its diff:
```python
import functools

import jax
import jax.numpy as jnp
from jax import lax
from jax.experimental import pallas as pl
from jax.experimental.pallas import tpu as pltpu
from jax.sharding import PartitionSpec as P

MESH = pl.DeviceIdType.MESH
F32 = jnp.float32
BF16 = jnp.bfloat16

LAG_MID, LAG_SUM, LAG_FWD, LAG_GRAD, LAG_ACC, LAG_OUT = 1, 3, 4, 6, 7, 7


def contract_cols(left, right):
    return lax.dot_general(left, right, (((1,), (1,)), ((), ())), preferred_element_type=F32)


def contract_rows(left, right):
    return lax.dot_general(left, right, (((0,), (0,)), ((), ())), preferred_element_type=F32)


def kernel(
    sizes,
    x_hbm, g_hbm, wg_hbm, wu_hbm, wd_hbm,
    od_hbm, og_hbm, ou_hbm, or_ref,
    wg, wu, wd, xg, part, opp_out, near_out, opp_in, near_in, mid_out, mid_in, h,
    acc_g, acc_u, acc_d, dg_out, dg_in, fin_out, fin_in, st_g, st_u, st_d,
    load_sem, store_sem,
    z_s, z_r, sib_s, sib_r, opp_s, opp_r, near_s, near_r, mid_s, mid_r, ag_s, ag_r, dg_s, dg_r, fin_s, fin_r,
):
    n_sec, n_row, n_col = sizes
    n_z = n_col // 2
    chunks = n_z
    tok = x_hbm.shape[1]
    span = 2 * tok
    quarter = span // n_row
    feat, width = wg.shape
    sec, row, col = lax.axis_index("section"), lax.axis_index("row"), lax.axis_index("col")
    core, z = col % 2, col // 2
    sibling = {"col": col + 1 - 2 * core}
    before = (sec + n_sec - 1) % n_sec
    after = (sec + 1) % n_sec

    def rows(start, size):
        return pl.ds(pl.multiple_of(start, size), size)

    def turn(k):
        return 1 - 2 * (k % 2)

    def at_row(shift):
        return (row + shift + n_row) % n_row

    def offset(k):
        return -((k + 1) // 2) * turn(k)

    def remote(src, dst, send, recv, device):
        return pltpu.make_async_remote_copy(
            src_ref=src, dst_ref=dst, send_sem=send, recv_sem=recv, device_id=device, device_id_type=MESH
        )

    own = rows(tok * core, tok)
    loads = [
        pltpu.make_async_copy(x_hbm.at[0], xg.at[0, own], load_sem.at[0]),
        pltpu.make_async_copy(g_hbm.at[0], xg.at[1, own], load_sem.at[1]),
        pltpu.make_async_copy(wg_hbm.at[0], wg, load_sem.at[2]),
        pltpu.make_async_copy(wu_hbm.at[0], wu, load_sem.at[3]),
        pltpu.make_async_copy(wd_hbm.at[0], wd, load_sem.at[4]),
    ]
    for load in loads:
        load.start()

    barrier = pltpu.get_barrier_semaphore()

    def greet(device):
        pl.semaphore_signal(barrier, inc=1, device_id=device, device_id_type=MESH)

    greet(sibling)
    greet({"row": at_row(1)})
    greet({"row": at_row(-1)})

    def greet_z(j, _):
        other = 2 * ((z + j) % n_z) + core

        @pl.when(j > 0)
        def _():
            greet({"col": other})

        greet({"section": before, "col": other})
        greet({"section": after, "col": other})
        return 0

    lax.fori_loop(0, n_z, greet_z, 0)

    acc_g[...] = jnp.zeros_like(acc_g)
    acc_u[...] = jnp.zeros_like(acc_u)
    acc_d[...] = jnp.zeros_like(acc_d)
    loads[0].wait()
    loads[1].wait()
    pl.semaphore_wait(barrier, 3 * n_z + 2)

    def to_sibling(k, half):
        place = rows(span * k + tok * half, tok)
        return remote(xg.at[:, place], xg.at[:, place], sib_s.at[k], sib_r.at[k], sibling)

    def along_z(k):
        place = rows(span * k + tok * core, tok)
        target = (z - offset(k) + n_z) % n_z
        return remote(xg.at[:, own], xg.at[:, place], z_s.at[k], z_r.at[k], {"col": 2 * target + core})

    def opp_copy(k):
        place = rows(quarter * k, quarter)
        return remote(opp_out.at[place], opp_in.at[place], opp_s.at[k], opp_r.at[k], {"row": at_row(turn(k))})

    def near_copy(k):
        place = rows(quarter * k, quarter)
        return remote(near_out.at[place], near_in.at[place], near_s.at[k], near_r.at[k], {"row": at_row(-turn(k))})

    def mid_copy(k):
        place = rows(quarter * k, quarter)
        return remote(mid_out.at[place], mid_in.at[place], mid_s.at[k], mid_r.at[k], {"row": at_row(turn(k))})

    def piece(k, owner):
        return rows(span * k + quarter * owner, quarter)

    def ag_copy(k, slot, owner, target):
        place = piece(k, owner)
        return remote(h.at[place], h.at[place], ag_s.at[3 * k + slot], ag_r.at[3 * k + slot], {"row": target})

    def dg_copy(k):
        return remote(dg_out.at[k], dg_in.at[k], dg_s.at[k], dg_r.at[k], sibling)

    def fin_copy(k):
        target = (z + offset(k) + n_z) % n_z
        return remote(
            fin_out.at[k], fin_in.at[k], fin_s.at[k], fin_r.at[k], {"section": before, "col": 2 * target + core}
        )

    def forward(k):
        to_sibling(k, 1 - core).wait_recv()
        place = rows(span * k, span)
        x, g = xg[0, place, :], xg[1, place, :]

        @pl.when(k == 0)
        def _():
            loads[2].wait()

        part[place, :width] = jnp.dot(x, wg[...], preferred_element_type=F32)

        @pl.when(k == 0)
        def _():
            loads[3].wait()

        part[place, width : 2 * width] = jnp.dot(x, wu[...], preferred_element_type=F32)

        @pl.when(k == 0)
        def _():
            loads[4].wait()

        part[place, 2 * width :] = contract_cols(g, wd[...])
        slot = rows(quarter * k, quarter)
        opp_out[slot] = part[piece(k, at_row(2)), :].astype(BF16)
        opp_copy(k).start()
        near_out[slot] = part[piece(k, at_row(-turn(k))), :].astype(BF16)
        near_copy(k).start()

    def middle(k):
        slot = rows(quarter * k, quarter)
        opp_copy(k).wait_recv()
        mid_out[slot] = (part[piece(k, at_row(turn(k))), :] + opp_in[slot].astype(F32)).astype(BF16)
        mid_copy(k).start()

    def sums(k):
        slot = rows(quarter * k, quarter)
        near_copy(k).wait_recv()
        mid_copy(k).wait_recv()
        mine = piece(k, row)
        total = part[mine, :] + near_in[slot].astype(F32) + mid_in[slot].astype(F32)
        gate, up, grad_hidden = total[:, :width], total[:, width : 2 * width], total[:, 2 * width :]
        sig = jax.nn.sigmoid(gate)
        h[mine, :width] = (grad_hidden * up * sig * (1.0 + gate * (1.0 - sig))).astype(BF16)
        h[mine, width : 2 * width] = (grad_hidden * gate * sig).astype(BF16)
        h[mine, 2 * width :] = (gate * sig * up).astype(BF16)
        ag_copy(k, 0, row, at_row(-turn(k))).start()
        ag_copy(k, 1, row, at_row(turn(k))).start()

    def onward(k):
        ag_copy(k, 0, at_row(turn(k)), row).wait_recv()
        ag_copy(k, 2, at_row(turn(k)), at_row(-turn(k))).start()

    def input_grad(k):
        ag_copy(k, 1, at_row(-turn(k)), row).wait_recv()
        ag_copy(k, 2, at_row(2), row).wait_recv()
        place = rows(span * k, span)
        part[place, :feat] = contract_cols(h[place, :width], wg[...]) + contract_cols(
            h[place, width : 2 * width], wu[...]
        )
        dg_out[k] = part[rows(span * k + tok * (1 - core), tok), :feat]
        dg_copy(k).start()

    def send_grad(k):
        dg_copy(k).wait_recv()
        fin_out[k] = (part[rows(span * k + tok * core, tok), :feat] + dg_in[k]).astype(BF16)
        fin_copy(k).start()

    def pair(k):
        return rows(span * (k - 1), 2 * span)

    def accumulate(k):
        place = pair(k)
        acc_g[...] += contract_rows(xg[0, place, :], h[place, :width])
        acc_u[...] += contract_rows(xg[0, place, :], h[place, width : 2 * width])
        acc_d[...] += contract_rows(h[place, 2 * width :], xg[1, place, :])

    def stage(i, lag, run, extra=None):
        k = i - lag
        ok = (k >= 0) & (k < chunks)
        if extra is not None:
            ok = ok & extra(k)

        @pl.when(ok)
        def _():
            run(k)

    to_sibling(0, core).start()
    along_z(1).start()
    along_z(2).start()

    def step(i, _):
        stage(i, 0, forward)

        @pl.when(i + 3 < chunks)
        def _():
            along_z(i + 3).start()

        stage(i, LAG_SUM, sums)
        stage(i, LAG_ACC, accumulate, lambda k: (k % 2 == 1) & (k < chunks - 1))
        stage(i, LAG_MID, middle)
        stage(i, LAG_OUT, send_grad)
        stage(i, LAG_GRAD, input_grad)
        stage(i, LAG_FWD, onward)

        @pl.when(i + 1 < chunks)
        def _():
            along_z(i + 1).wait_recv()
            to_sibling(i + 1, core).start()

        return 0

    lax.fori_loop(0, chunks + LAG_GRAD, step, 0)

    last = chunks - 1
    place = pair(last)
    st_g[...] = (acc_g[...] + contract_rows(xg[0, place, :], h[place, :width])).astype(BF16)
    stores = [
        pltpu.make_async_copy(st_g, og_hbm.at[0], store_sem.at[0]),
        pltpu.make_async_copy(st_u, ou_hbm.at[0], store_sem.at[1]),
        pltpu.make_async_copy(st_d, od_hbm.at[0], store_sem.at[2]),
    ]
    stores[0].start()
    send_grad(last)
    st_u[...] = (acc_u[...] + contract_rows(xg[0, place, :], h[place, width : 2 * width])).astype(BF16)
    stores[1].start()
    st_d[...] = (acc_d[...] + contract_rows(h[place, 2 * width :], xg[1, place, :])).astype(BF16)
    stores[2].start()

    def sent(k, _):
        @pl.when(k > 0)
        def _():
            along_z(k).wait_send()

        to_sibling(k, core).wait_send()
        opp_copy(k).wait_send()
        near_copy(k).wait_send()
        mid_copy(k).wait_send()
        ag_copy(k, 0, row, at_row(-turn(k))).wait_send()
        ag_copy(k, 1, row, at_row(turn(k))).wait_send()
        ag_copy(k, 2, at_row(turn(k)), at_row(-turn(k))).wait_send()
        dg_copy(k).wait_send()
        fin_copy(k).wait_send()
        fin_copy(k).wait_recv()
        return 0

    lax.fori_loop(0, chunks, sent, 0)
    total = fin_in[0].astype(F32)
    for k in range(1, chunks):
        total = total + fin_in[k].astype(F32)
    or_ref[0] = total.astype(BF16)
    for store in stores:
        store.wait()


def shards(sizes, layer_input, output_grad, gate_weight, up_weight, down_weight):
    tok, feat = layer_input.shape[1:]
    width = gate_weight.shape[2]
    chunks = sizes[2] // 2
    span = 2 * tok
    total = span * chunks
    quarter_rows = total // sizes[1]
    dma = pltpu.SemaphoreType.DMA
    shapes = [
        jax.ShapeDtypeStruct((1, width, feat), BF16),
        jax.ShapeDtypeStruct((1, feat, width), BF16),
        jax.ShapeDtypeStruct((1, feat, width), BF16),
        jax.ShapeDtypeStruct((1, tok, feat), BF16),
    ]
    return pl.pallas_call(
        functools.partial(kernel, sizes),
        out_shape=shapes,
        in_specs=[pl.BlockSpec(memory_space=pl.ANY)] * 5,
        out_specs=[pl.BlockSpec(memory_space=pl.ANY)] * 3 + [pl.BlockSpec(memory_space=pltpu.VMEM)],
        scratch_shapes=[
            pltpu.VMEM((feat, width), BF16),
            pltpu.VMEM((feat, width), BF16),
            pltpu.VMEM((width, feat), BF16),
            pltpu.VMEM((2, total, feat), BF16),
            pltpu.VMEM((total, 3 * width), F32),
        ]
        + [pltpu.VMEM((quarter_rows, 3 * width), BF16)] * 6
        + [
            pltpu.VMEM((total, 3 * width), BF16),
            pltpu.VMEM((feat, width), F32),
            pltpu.VMEM((feat, width), F32),
            pltpu.VMEM((width, feat), F32),
            pltpu.VMEM((chunks, tok, feat), F32),
            pltpu.VMEM((chunks, tok, feat), F32),
            pltpu.VMEM((chunks, tok, feat), BF16),
            pltpu.VMEM((chunks, tok, feat), BF16),
            pltpu.VMEM((feat, width), BF16),
            pltpu.VMEM((feat, width), BF16),
            pltpu.VMEM((width, feat), BF16),
            dma((5,)),
            dma((3,)),
        ]
        + [dma((chunks,))] * 10
        + [dma((3 * chunks,))] * 2
        + [dma((chunks,))] * 4,
        compiler_params=pltpu.CompilerParams(
            collective_id=0, has_side_effects=True, vmem_limit_bytes=58 * 1024 * 1024
        ),
    )(layer_input, output_grad, gate_weight, up_weight, down_weight)


def solution(mesh):
    sizes = tuple(mesh.shape[axis] for axis in ("section", "row", "col"))
    return jax.shard_map(
        functools.partial(shards, sizes),
        mesh=mesh,
        in_specs=(
            P("section", "col", "row"),
            P("section", "col", "row"),
            P("section", "row", "col"),
            P("section", "row", "col"),
            P("section", "col", "row"),
        ),
        out_specs=(
            P("section", "col", "row"),
            P("section", "row", "col"),
            P("section", "row", "col"),
            P("section", "col", "row"),
        ),
        check_vma=False,
    )
```

time: 272 us -> 86.7 us (0.32)
  waiting for transfers between devices: 182 us -> 0 us
  Pallas kernels: 0 us -> 78 us
  blocking collectives: 33.5 us -> 0 us
  matrix products: 23.4 us -> 0 us
  between operations: 13.8 us -> 0.65 us
  other arithmetic: 5.24 us -> 0 us
    reduce_scatter x2 -> x0, waiting for transfers between devices: 104 us -> none  [the longest x1 58.5 us: shards(): lax.psum_scatter(jnp.concatenate([jnp.dot(in_rows, w_gate, preferred_elem...]
    pallas_call x0 -> x1, Pallas kernels: none -> 78 us  [shards(): pl.pallas_call(functools.partial(kernel, sizes), out_shape=shapes, in_spe...]
    all_gather x2 -> x0, waiting for transfers between devices: 76.7 us -> none  [the longest x1 44 us: shards(): lax.all_gather(inputs, 'col', axis=0, tiled=True)]
    all_gather x3 -> x0, blocking collectives: 33.5 us -> none  [the longest x1 11.7 us: shards(): grad_gate_in = lax.all_gather(pieces[1], 'row', axis=0, tiled=True)]
    dot_general x8 -> x0, matrix products: 23.4 us -> none  [the longest x3 9.94 us: contract_rows(): lax.dot_general(left, right, (((0,), (0,)), ((), ())), preferred_element_...]
    concatenate x1 -> x0, other arithmetic: 2.77 us -> none  [shards(): jnp.concatenate([jnp.dot(in_rows, w_gate, preferred_element_type=jnp.floa...]
    unnamed x19 -> x10, local copies, waits for them, and re-layouts: 8.8 us -> 7.03 us
  transfers between devices with their start and end apart: 5 -> 0, of which waited for: 4 -> 0; matrix products, arithmetic and copies ran while one was open for 9% -> 0% of each run, Pallas kernels for 0% -> 0%
where the time goes in v1:
time: 86.7 us; the launch traced here: 85.7 us
  Pallas kernels  78 us (90%)
  local copies, waits for them, and re-layouts  7.03 us (8%)
    pallas_call x1, Pallas kernels, shards(): pl.pallas_call(functools.partial(kernel, sizes), out_shape=shapes, in_spe...  78 us
    unnamed x10, local copies, waits for them, and re-layouts  7.03 us

profile of v1, /device:TPU:1, one launch (start us, length us, event | category | flops | bytes accessed | tf_op | source)
XLA Modules:
  0.0 85.7 jit_solution(7749851873121395746)
XLA Ops:
  0.6 78.0 %shard_map.84 = (bf16[1,896,1024]{2,1,0:T(8,128)(2,1)}, bf16[1,1024,896]{2,1,0:T(8,128)(2,1)}, bf16[1,1024,896]{2,1,0:T(8,128)(2,1)}, bf16[1,32,1024]{2,1,0:T(8,128)(2,1)}) custom-call(bf16[1,32,1024]{2,1,0:T(8,128)(2,1)} %x_hbm.1, bf16[1,32,1024]{2,1,0:T(8,128)(2,1)} %g_hbm.1, bf16[1,1024,896]{2,1,0:T(8,128)(2,1)} %wg_hbm.1, bf16[1,1024,896]{2,1,0:T(8,128)(2,1)} %wu_hbm.1, ...), custom_call_target="tpu_custom_call" | custom-call | tf_op jit(solution)/shard_map/pallas_call | solution.py:309
  78.6 0.0 copy-start.1
  78.6 3.0 %copy.13 = bf16[1,896,1024]{2,1,0:T(8,128)(2,1)} copy(bf16[1,896,1024]{2,1,0:T(8,128)(2,1)} %get-tuple-element.8) | data formatting | bytes 3670016
  81.6 0.0 copy-done.1
  81.6 0.0 copy-start
  81.7 1.2 %copy.14 = bf16[1,1024,896]{2,1,0:T(8,128)(2,1)} copy(bf16[1,1024,896]{2,1,0:T(8,128)(2,1)S(1)} %copy-done.1) | data formatting | bytes 3670016
  82.9 0.9 %copy-done = bf16[1,1024,896]{2,1,0:T(8,128)(2,1)S(1)} copy-done((bf16[1,1024,896]{2,1,0:T(8,128)(2,1)S(1)}, bf16[1,1024,896]{2,1,0:T(8,128)(2,1)}, u32[]{:S(2)}) %copy-start) | copy-done | bytes 1835032
  83.8 0.0 copy-start.2
  83.8 1.2 %copy.15 = bf16[1,1024,896]{2,1,0:T(8,128)(2,1)} copy(bf16[1,1024,896]{2,1,0:T(8,128)(2,1)S(1)} %copy-done) | data formatting | bytes 3670016
  85.0 0.0 copy-done.2
  85.0 0.6 copy.16
Async XLA Ops:
  78.6 3.0 %copy-start.1 = (bf16[1,1024,896]{2,1,0:T(8,128)(2,1)S(1)}, bf16[1,1024,896]{2,1,0:T(8,128)(2,1)}, u32[]{:S(2)}) copy-start(bf16[1,1024,896]{2,1,0:T(8,128)(2,1)} %get-tuple-element.9) | copy-start | bytes 5505028
  81.6 2.2 %copy-start = (bf16[1,1024,896]{2,1,0:T(8,128)(2,1)S(1)}, bf16[1,1024,896]{2,1,0:T(8,128)(2,1)}, u32[]{:S(2)}) copy-start(bf16[1,1024,896]{2,1,0:T(8,128)(2,1)} %get-tuple-element.10) | copy-start | bytes 5505028
  83.8 1.2 %copy-start.2 = (bf16[1,32,1024]{2,1,0:T(8,128)(2,1)S(1)}, bf16[1,32,1024]{2,1,0:T(8,128)(2,1)}, u32[]{:S(2)}) copy-start(bf16[1,32,1024]{2,1,0:T(8,128)(2,1)} %get-tuple-element.11) | copy-start | bytes 196612

commit v2 on v1

v2 whole, which is shorter than its diff:
```python
import functools

import jax
import jax.numpy as jnp
from jax import lax
from jax.experimental import pallas as pl
from jax.experimental.pallas import tpu as pltpu
from jax.sharding import PartitionSpec as P

MESH = pl.DeviceIdType.MESH
F32 = jnp.float32
BF16 = jnp.bfloat16

LAG_MID, LAG_SUM, LAG_FWD, LAG_GRAD, LAG_ACC, LAG_OUT = 2, 4, 6, 9, 9, 10
LAG_HID, LAG_HID_FWD, LAG_DOWN = 9, 13, 21


def contract_cols(left, right):
    return lax.dot_general(left, right, (((1,), (1,)), ((), ())), preferred_element_type=F32)


def contract_rows(left, right):
    return lax.dot_general(left, right, (((0,), (0,)), ((), ())), preferred_element_type=F32)


def kernel(
    sizes,
    x_hbm, g_hbm, wg_hbm, wu_hbm, wd_hbm,
    st_d, st_g, st_u, or_ref,
    wg, wu, wd, xg, part, opp_out, near_out, opp_in, near_in, mid_out, mid_in, h, hid,
    acc_g, acc_u, acc_d, dg_out, dg_in, fin_out, fin_in,
    load_sem, go_sem,
    z_s, z_r, sib_s, sib_r, opp_s, opp_r, near_s, near_r, mid_s, mid_r, ag_s, ag_r, hid_s, hid_r, dg_s, dg_r, fin_s, fin_r,
):
    n_sec, n_row, n_col = sizes
    n_z = n_col // 2
    chunks = n_z
    tok = x_hbm.shape[1]
    span = 2 * tok
    quarter = span // n_row
    feat, width = wg.shape
    sec, row, col = lax.axis_index("section"), lax.axis_index("row"), lax.axis_index("col")
    core, z = col % 2, col // 2
    sibling = {"col": col + 1 - 2 * core}
    before = (sec + n_sec - 1) % n_sec
    after = (sec + 1) % n_sec

    def rows(start, size):
        return pl.ds(pl.multiple_of(start, size), size)

    def turn(k):
        return 1 - 2 * (k % 2)

    def at_row(shift):
        return (row + shift + n_row) % n_row

    def at_z(shift):
        return 2 * ((z + shift + n_z) % n_z) + core

    def offset(k):
        return -((k + 1) // 2) * turn(k)

    def remote(src, dst, send, recv, device):
        return pltpu.make_async_remote_copy(
            src_ref=src, dst_ref=dst, send_sem=send, recv_sem=recv, device_id=device, device_id_type=MESH
        )

    own = rows(tok * core, tok)
    loads = [
        pltpu.make_async_copy(x_hbm.at[0], xg.at[0, own], load_sem.at[0]),
        pltpu.make_async_copy(g_hbm.at[0], xg.at[1, own], load_sem.at[1]),
        pltpu.make_async_copy(wg_hbm.at[0], wg, load_sem.at[2]),
        pltpu.make_async_copy(wu_hbm.at[0], wu, load_sem.at[3]),
        pltpu.make_async_copy(wd_hbm.at[0], wd, load_sem.at[4]),
    ]
    for load in loads:
        load.start()

    barrier = pltpu.get_barrier_semaphore()

    def greet(device):
        pl.semaphore_signal(barrier, inc=1, device_id=device, device_id_type=MESH)

    greet(sibling)
    greet({"row": at_row(1)})
    greet({"row": at_row(-1)})

    greet({"section": before})
    greet({"section": after})

    greet({"col": at_z(1)})
    greet({"col": at_z(-1)})

    acc_g[...] = jnp.zeros_like(acc_g)
    acc_u[...] = jnp.zeros_like(acc_u)
    acc_d[...] = jnp.zeros_like(acc_d)
    loads[0].wait()
    loads[1].wait()
    pl.semaphore_wait(barrier, 7)

    def to_sibling(k, half):
        place = rows(span * k + tok * half, tok)
        return remote(xg.at[:, place], xg.at[:, place], sib_s.at[k], sib_r.at[k], sibling)

    def along_z(k):
        held = rows(span * jnp.maximum(k - 2, 0) + tok * core, tok)
        place = rows(span * k + tok * core, tok)
        return remote(xg.at[:, held], xg.at[:, place], z_s.at[k], z_r.at[k], {"col": at_z(turn(k))})

    def pass_on(k):
        along_z(k).wait_recv()

        @pl.when(k + 2 < chunks)
        def _():
            along_z(k + 2).start()

        to_sibling(k, core).start()

    def opp_copy(k):
        place = rows(quarter * k, quarter)
        return remote(opp_out.at[place], opp_in.at[place], opp_s.at[k], opp_r.at[k], {"row": at_row(turn(k))})

    def near_copy(k):
        place = rows(quarter * k, quarter)
        return remote(near_out.at[place], near_in.at[place], near_s.at[k], near_r.at[k], {"row": at_row(-turn(k))})

    def mid_copy(k):
        place = rows(quarter * k, quarter)
        return remote(mid_out.at[place], mid_in.at[place], mid_s.at[k], mid_r.at[k], {"row": at_row(turn(k))})

    def piece(k, owner):
        return rows(span * k + quarter * owner, quarter)

    def ag_copy(k, slot, owner, target):
        place = piece(k, owner)
        return remote(h.at[place], h.at[place], ag_s.at[3 * k + slot], ag_r.at[3 * k + slot], {"row": target})

    def hid_copy(k, slot, owner, target):
        place = piece(k, owner)
        return remote(hid.at[place], hid.at[place], hid_s.at[3 * k + slot], hid_r.at[3 * k + slot], {"row": target})

    def dg_copy(k):
        return remote(dg_out.at[k], dg_in.at[k], dg_s.at[k], dg_r.at[k], sibling)

    def fin_copy(k):
        target = {"section": before, "col": at_z(offset(k))}
        return remote(fin_out.at[k], fin_in.at[k], fin_s.at[k], fin_r.at[k], target)

    def forward(k):
        to_sibling(k, 1 - core).wait_recv()
        place = rows(span * k, span)
        x, g = xg[0, place, :], xg[1, place, :]

        @pl.when(k == 0)
        def _():
            loads[2].wait()

        part[place, :width] = jnp.dot(x, wg[...], preferred_element_type=F32)

        @pl.when(k == 0)
        def _():
            loads[3].wait()

        part[place, width : 2 * width] = jnp.dot(x, wu[...], preferred_element_type=F32)

        @pl.when(k == 0)
        def _():
            loads[4].wait()

        part[place, 2 * width :] = contract_cols(g, wd[...])
        slot = rows(quarter * k, quarter)
        opp_out[slot] = part[piece(k, at_row(2)), :].astype(BF16)
        opp_copy(k).start()
        near_out[slot] = part[piece(k, at_row(-turn(k))), :].astype(BF16)
        near_copy(k).start()

    def middle(k):
        slot = rows(quarter * k, quarter)
        opp_copy(k).wait_recv()
        mid_out[slot] = (part[piece(k, at_row(turn(k))), :] + opp_in[slot].astype(F32)).astype(BF16)
        mid_copy(k).start()

    def sums(k):
        slot = rows(quarter * k, quarter)
        near_copy(k).wait_recv()
        mid_copy(k).wait_recv()
        mine = piece(k, row)
        total = part[mine, :] + near_in[slot].astype(F32) + mid_in[slot].astype(F32)
        gate, up, grad_hidden = total[:, :width], total[:, width : 2 * width], total[:, 2 * width :]
        sig = jax.nn.sigmoid(gate)
        h[mine, :width] = (grad_hidden * up * sig * (1.0 + gate * (1.0 - sig))).astype(BF16)
        h[mine, width : 2 * width] = (grad_hidden * gate * sig).astype(BF16)
        hid[mine, :] = (gate * sig * up).astype(BF16)
        ag_copy(k, 0, row, at_row(-turn(k))).start()
        ag_copy(k, 1, row, at_row(turn(k))).start()

    def onward(k):
        ag_copy(k, 0, at_row(turn(k)), row).wait_recv()
        ag_copy(k, 2, at_row(turn(k)), at_row(-turn(k))).start()

    def hidden_out(k):
        hid_copy(k, 0, row, at_row(-turn(k))).start()
        hid_copy(k, 1, row, at_row(turn(k))).start()

    def hidden_onward(k):
        hid_copy(k, 0, at_row(turn(k)), row).wait_recv()
        hid_copy(k, 2, at_row(turn(k)), at_row(-turn(k))).start()
        opp_copy(k).wait_send()
        near_copy(k).wait_send()
        mid_copy(k).wait_send()
        ag_copy(k, 0, row, at_row(-turn(k))).wait_send()
        ag_copy(k, 1, row, at_row(turn(k))).wait_send()

    def hidden_in(k):
        hid_copy(k, 1, at_row(-turn(k)), row).wait_recv()
        hid_copy(k, 2, at_row(2), row).wait_recv()
        ag_copy(k, 2, at_row(turn(k)), at_row(-turn(k))).wait_send()
        hid_copy(k, 0, row, at_row(-turn(k))).wait_send()
        hid_copy(k, 1, row, at_row(turn(k))).wait_send()
        hid_copy(k, 2, at_row(turn(k)), at_row(-turn(k))).wait_send()

    def pair(k):
        return rows(span * (k - 1), 2 * span)

    def input_grad(k):
        for q in (k - 1, k):
            ag_copy(q, 1, at_row(-turn(q)), row).wait_recv()
            ag_copy(q, 2, at_row(2), row).wait_recv()
        place = pair(k)
        part[place, :feat] = contract_cols(h[place, :width], wg[...]) + contract_cols(h[place, width:], wu[...])
        for q in (k - 1, k):
            dg_out[q] = part[rows(span * q + tok * (1 - core), tok), :feat]
            dg_copy(q).start()

    def send_grad(k):
        @pl.when(k == 1)
        def _():
            pl.semaphore_wait(go_sem, 1)

        for q in (k - 1, k):
            dg_copy(q).wait_recv()
            fin_out[q] = (part[rows(span * q + tok * core, tok), :feat] + dg_in[q]).astype(BF16)
            fin_copy(q).start()
        for q in (k - 1, k):
            dg_copy(q).wait_send()
            to_sibling(q, core).wait_send()

            @pl.when(q > 0)
            def _():
                along_z(q).wait_send()

    def accumulate(k):
        place = pair(k)
        acc_g[...] += contract_rows(xg[0, place, :], h[place, :width])
        acc_u[...] += contract_rows(xg[0, place, :], h[place, width:])

    def finish(k):
        place = pair(k)
        st_g[0] = (acc_g[...] + contract_rows(xg[0, place, :], h[place, :width])).astype(BF16)
        st_u[0] = (acc_u[...] + contract_rows(xg[0, place, :], h[place, width:])).astype(BF16)

    def accumulate_down(k):
        place = pair(k)
        acc_d[...] += contract_rows(hid[place, :], xg[1, place, :])

    def stage(i, lag, run, extra=None):
        k = i - lag
        ok = (k >= 0) & (k < chunks)
        if extra is not None:
            ok = ok & extra(k)

        @pl.when(ok)
        def _():
            run(k)

    along_z(1).start()
    along_z(2).start()
    to_sibling(0, core).start()

    last = chunks - 1

    def odd(k):
        return k % 2 == 1

    def odd_not_last(k):
        return (k % 2 == 1) & (k < last)

    def step(i, _):
        stage(i, LAG_MID, middle)
        stage(i, LAG_OUT, send_grad, odd)
        stage(i, 0, forward)
        stage(i, LAG_HID_FWD, hidden_onward)
        stage(i, LAG_HID, hidden_out)
        stage(i, LAG_DOWN, hidden_in)
        stage(i, LAG_DOWN, accumulate_down, odd_not_last)
        stage(i, LAG_GRAD, input_grad, odd)
        stage(i, LAG_SUM, sums)
        stage(i, LAG_ACC, accumulate, odd_not_last)
        stage(i, LAG_ACC, finish, lambda k: k == last)
        stage(i, -1, pass_on, lambda k: k > 0)

        @pl.when(i == chunks - 2)
        def _():
            pl.semaphore_signal(go_sem, inc=1, device_id={"section": after}, device_id_type=MESH)

        stage(i, LAG_FWD, onward)
        return 0

    lax.fori_loop(0, chunks + LAG_DOWN, step, 0)

    place = pair(last)
    st_d[0] = (acc_d[...] + contract_rows(hid[place, :], xg[1, place, :])).astype(BF16)
    for k in range(chunks):
        fin_copy(k).wait_recv()
        fin_copy(k).wait_send()
    total = fin_in[0].astype(F32)
    for k in range(1, chunks):
        total = total + fin_in[k].astype(F32)
    or_ref[0] = total.astype(BF16)


def write_out(d_in, g_in, u_in, r_in, d_out, g_out, u_out, r_out, sem):
    pairs = [(d_in, d_out), (g_in, g_out), (u_in, u_out), (r_in, r_out)]
    copies = [pltpu.make_async_copy(src, dst, sem.at[j]) for j, (src, dst) in enumerate(pairs)]
    for copy in copies:
        copy.start()
    for copy in copies:
        copy.wait()


def shards(sizes, layer_input, output_grad, gate_weight, up_weight, down_weight):
    tok, feat = layer_input.shape[1:]
    width = gate_weight.shape[2]
    chunks = sizes[2] // 2
    span = 2 * tok
    total = span * chunks
    quarter_rows = total // sizes[1]
    dma = pltpu.SemaphoreType.DMA
    shapes = [(1, width, feat), (1, feat, width), (1, feat, width), (1, tok, feat)]
    results = pl.pallas_call(
        functools.partial(kernel, sizes),
        out_shape=[pltpu.VMEM(shape, BF16) for shape in shapes],
        in_specs=[pl.BlockSpec(memory_space=pltpu.HBM)] * 5,
        out_specs=[pl.BlockSpec(memory_space=pltpu.VMEM)] * 4,
        scratch_shapes=[
            pltpu.VMEM((feat, width), BF16),
            pltpu.VMEM((feat, width), BF16),
            pltpu.VMEM((width, feat), BF16),
            pltpu.VMEM((2, total, feat), BF16),
            pltpu.VMEM((total, 3 * width), F32),
        ]
        + [pltpu.VMEM((quarter_rows, 3 * width), BF16)] * 6
        + [
            pltpu.VMEM((total, 2 * width), BF16),
            pltpu.VMEM((total, width), BF16),
            pltpu.VMEM((feat, width), F32),
            pltpu.VMEM((feat, width), F32),
            pltpu.VMEM((width, feat), F32),
            pltpu.VMEM((chunks, tok, feat), F32),
            pltpu.VMEM((chunks, tok, feat), F32),
            pltpu.VMEM((chunks, tok, feat), BF16),
            pltpu.VMEM((chunks, tok, feat), BF16),
            dma((5,)),
            pltpu.SemaphoreType.REGULAR,
        ]
        + [dma((chunks,))] * 10
        + [dma((3 * chunks,))] * 4
        + [dma((chunks,))] * 4,
        compiler_params=pltpu.CompilerParams(
            collective_id=0, has_side_effects=True, vmem_limit_bytes=57 * 1024 * 1024
        ),
    )(layer_input, output_grad, gate_weight, up_weight, down_weight)
    return pl.pallas_call(
        write_out,
        out_shape=[jax.ShapeDtypeStruct(shape, BF16) for shape in shapes],
        in_specs=[pl.BlockSpec(memory_space=pl.ANY)] * 4,
        out_specs=[pl.BlockSpec(memory_space=pltpu.HBM)] * 4,
        scratch_shapes=[dma((4,))],
        compiler_params=pltpu.CompilerParams(vmem_limit_bytes=1024 * 1024),
    )(*results)


def solution(mesh):
    sizes = tuple(mesh.shape[axis] for axis in ("section", "row", "col"))
    return jax.shard_map(
        functools.partial(shards, sizes),
        mesh=mesh,
        in_specs=(
            P("section", "col", "row"),
            P("section", "col", "row"),
            P("section", "row", "col"),
            P("section", "row", "col"),
            P("section", "col", "row"),
        ),
        out_specs=(
            P("section", "col", "row"),
            P("section", "row", "col"),
            P("section", "row", "col"),
            P("section", "col", "row"),
        ),
        check_vma=False,
    )
```

time: 86.7 us -> 73.8 us (0.85); the launches traced: 85.7 us -> 73.8 us
  local copies, waits for them, and re-layouts: 7.03 us -> 0 us
  Pallas kernels: 78 us -> 73.1 us
    unnamed x10 -> x0, local copies, waits for them, and re-layouts: 7.03 us -> none
    pallas_call x1 -> x2, Pallas kernels: 78 us -> 73.1 us  [the longest x1 70.6 us: shards(): pl.pallas_call(functools.partial(kernel, sizes), out_shape=[pltpu.VMEM(sh...]
where the time goes in v2:
time: 73.8 us
  Pallas kernels  73.1 us (99%)
    pallas_call x1, Pallas kernels, shards(): pl.pallas_call(functools.partial(kernel, sizes), out_shape=[pltpu.VMEM(sh...  70.6 us
    pallas_call x1, Pallas kernels, shards(): pl.pallas_call(write_out, out_shape=[jax.ShapeDtypeStruct(shape, BF16) fo...  2.48 us

profile of v2, /device:TPU:1, one launch (start us, length us, event | category | flops | bytes accessed | tf_op | source)
XLA Modules:
  0.0 73.8 jit_solution(4962077918531023149)
XLA Ops:
  0.6 70.6 %shard_map.84 = (bf16[1,896,1024]{2,1,0:T(8,128)(2,1)S(1)}, bf16[1,1024,896]{2,1,0:T(8,128)(2,1)S(1)}, bf16[1,1024,896]{2,1,0:T(8,128)(2,1)S(1)}, bf16[1,32,1024]{2,1,0:T(8,128)(2,1)S(1)}) custom-call(bf16[1,32,1024]{2,1,0:T(8,128)(2,1)} %x_hbm.1, bf16[1,32,1024]{2,1,0:T(8,128)(2,1)} %g_hbm.1, bf16[1,1024,896]{2,1,0:T(8,128)(2,1)} %wg_hbm.1, ...), custom_call_target="tpu_custom_call" | custom-call | tf_op jit(solution)/shard_map/pallas_call | solution.py:340
  71.3 2.5 %shard_map.85 = (bf16[1,896,1024]{2,1,0:T(8,128)(2,1)}, bf16[1,1024,896]{2,1,0:T(8,128)(2,1)}, bf16[1,1024,896]{2,1,0:T(8,128)(2,1)}, bf16[1,32,1024]{2,1,0:T(8,128)(2,1)}) custom-call(bf16[1,896,1024]{2,1,0:T(8,128)(2,1)S(1)} %get-tuple-element.8.d_in, bf16[1,1024,896]{2,1,0:T(8,128)(2,1)S(1)} %get-tuple-element.9.g_in, ...), custom_call_target="tpu_custom_call" | custom-call | tf_op jit(solution)/shard_map/pallas_call | solution.py:373

commit v3 on v2

--- a/solution.py
+++ b/solution.py
@@ -11,8 +11,10 @@
 F32 = jnp.float32
 BF16 = jnp.bfloat16
 
-LAG_MID, LAG_SUM, LAG_FWD, LAG_GRAD, LAG_ACC, LAG_OUT = 2, 4, 6, 9, 9, 10
-LAG_HID, LAG_HID_FWD, LAG_DOWN = 9, 13, 21
+LAG_MID, LAG_SUM, LAG_FWD, LAG_GRAD, LAG_ACC, LAG_OUT = 2, 6, 8, 11, 11, 12
+LAG_HID, LAG_HID_FWD, LAG_DOWN = 13, 16, 23
+
+FIRST = 2
 
 
 def contract_cols(left, right):
@@ -233,10 +235,6 @@
             dg_copy(q).start()
 
     def send_grad(k):
-        @pl.when(k == 1)
-        def _():
-            pl.semaphore_wait(go_sem, 1)
-
         for q in (k - 1, k):
             dg_copy(q).wait_recv()
             fin_out[q] = (part[rows(span * q + tok * core, tok), :feat] + dg_in[q]).astype(BF16)
@@ -263,7 +261,10 @@
         place = pair(k)
         acc_d[...] += contract_rows(hid[place, :], xg[1, place, :])
 
-    def stage(i, lag, run, extra=None):
+    def in_turn(k):
+        return (k + FIRST) % chunks
+
+    def stage(i, lag, run, extra=None, turned=False):
         k = i - lag
         ok = (k >= 0) & (k < chunks)
         if extra is not None:
@@ -271,7 +272,7 @@
 
         @pl.when(ok)
         def _():
-            run(k)
+            run(in_turn(k) if turned else k)
 
     along_z(1).start()
     along_z(2).start()
@@ -279,6 +280,9 @@
 
     last = chunks - 1
 
+    def may_send(k):
+        pl.semaphore_wait(go_sem, 1)
+
     def odd(k):
         return k % 2 == 1
 
@@ -287,28 +291,29 @@
 
     def step(i, _):
         stage(i, LAG_MID, middle)
-        stage(i, LAG_OUT, send_grad, odd)
+        stage(i, LAG_OUT, may_send, lambda k: k == 1)
+        stage(i, LAG_OUT, send_grad, odd, True)
         stage(i, 0, forward)
-        stage(i, LAG_HID_FWD, hidden_onward)
-        stage(i, LAG_HID, hidden_out)
-        stage(i, LAG_DOWN, hidden_in)
-        stage(i, LAG_DOWN, accumulate_down, odd_not_last)
-        stage(i, LAG_GRAD, input_grad, odd)
-        stage(i, LAG_SUM, sums)
-        stage(i, LAG_ACC, accumulate, odd_not_last)
-        stage(i, LAG_ACC, finish, lambda k: k == last)
+        stage(i, LAG_HID_FWD, hidden_onward, None, True)
+        stage(i, LAG_HID, hidden_out, None, True)
+        stage(i, LAG_DOWN, hidden_in, None, True)
+        stage(i, LAG_DOWN, accumulate_down, odd_not_last, True)
+        stage(i, LAG_GRAD, input_grad, odd, True)
+        stage(i, LAG_SUM, sums, None, True)
+        stage(i, LAG_ACC, accumulate, odd_not_last, True)
+        stage(i, LAG_ACC, finish, lambda k: k == last, True)
         stage(i, -1, pass_on, lambda k: k > 0)
 
         @pl.when(i == chunks - 2)
         def _():
             pl.semaphore_signal(go_sem, inc=1, device_id={"section": after}, device_id_type=MESH)
 
-        stage(i, LAG_FWD, onward)
+        stage(i, LAG_FWD, onward, None, True)
         return 0
 
     lax.fori_loop(0, chunks + LAG_DOWN, step, 0)
 
-    place = pair(last)
+    place = pair(in_turn(last))
     st_d[0] = (acc_d[...] + contract_rows(hid[place, :], xg[1, place, :])).astype(BF16)
     for k in range(chunks):
         fin_copy(k).wait_recv()

time: 73.8 us -> 73.3 us (level)
  no operation moved by 1% of the time
where the time goes in v3:
time: 73.3 us; the launch traced here: 73.2 us
  Pallas kernels  72.6 us (99%)
    pallas_call x1, Pallas kernels, shards(): pl.pallas_call(functools.partial(kernel, sizes), out_shape=[pltpu.VMEM(sh...  70.1 us
    pallas_call x1, Pallas kernels, shards(): pl.pallas_call(write_out, out_shape=[jax.ShapeDtypeStruct(shape, BF16) fo...  2.48 us

profile of v3, /device:TPU:1, one launch (start us, length us, event | category | flops | bytes accessed | tf_op | source)
XLA Modules:
  0.0 73.2 jit_solution(15322601768492594555)
XLA Ops:
  0.6 70.1 %shard_map.84 = (bf16[1,896,1024]{2,1,0:T(8,128)(2,1)S(1)}, bf16[1,1024,896]{2,1,0:T(8,128)(2,1)S(1)}, bf16[1,1024,896]{2,1,0:T(8,128)(2,1)S(1)}, bf16[1,32,1024]{2,1,0:T(8,128)(2,1)S(1)}) custom-call(bf16[1,32,1024]{2,1,0:T(8,128)(2,1)} %x_hbm.1, bf16[1,32,1024]{2,1,0:T(8,128)(2,1)} %g_hbm.1, bf16[1,1024,896]{2,1,0:T(8,128)(2,1)} %wg_hbm.1, ...), custom_call_target="tpu_custom_call" | custom-call | tf_op jit(solution)/shard_map/pallas_call | solution.py:345
  70.8 2.5 %shard_map.85 = (bf16[1,896,1024]{2,1,0:T(8,128)(2,1)}, bf16[1,1024,896]{2,1,0:T(8,128)(2,1)}, bf16[1,1024,896]{2,1,0:T(8,128)(2,1)}, bf16[1,32,1024]{2,1,0:T(8,128)(2,1)}) custom-call(bf16[1,896,1024]{2,1,0:T(8,128)(2,1)S(1)} %get-tuple-element.8.d_in, bf16[1,1024,896]{2,1,0:T(8,128)(2,1)S(1)} %get-tuple-element.9.g_in, ...), custom_call_target="tpu_custom_call" | custom-call | tf_op jit(solution)/shard_map/pallas_call | solution.py:378
